TPU v7x, 32 devices: a whole 2x2x4 slice. The times are simulated.
32 devices in a mesh: dp: 8 (over z, y), block: 4 (over x, core).
Axes of the slice: x: 2, y: 2, z: 4, core: 2. Of those that a mesh axis runs over, the one named last changes fastest.
Arguments:
- x_act: bfloat16 [4, 4096, 4096], P('block', 'dp')
- g_out: bfloat16 [4, 4096, 4096], P('block', 'dp')
- proj_in: bfloat16 [4, 4096, 64], P('block'), may hold values from -0.09375 to 0.09375
- proj_out: bfloat16 [4, 4096, 64], P('block'), may hold values from -0.09375 to 0.09375
- queries: bfloat16 [4, 512, 4096], P('block', 'dp'), may hold values from -6 to 6
- cand_ids: int32 [8, 8, 2], P('dp'), may hold values from 0 to 15, as said below
- cand_counts: int32 [8, 8], P('dp'), may hold values from 0 to 2, as said below
Outputs:
- scores: float32 [512, 32], P(('dp', 'block'))
Inputs may be any that keep to these rules, and one draw needn't show every extreme that they name: `cand_ids`: each list of a training shard d for an owner p names 2 distinct query blocks of p; slots at or past cand_counts[d, p] are padding. Every training shard d has cand_counts[d, d] = 2.
All inputs are finite; a program needn't handle non-finite values.
Results may differ from a plain program's by a relative error of at most 0.0096.
Values may be sent and summed in bfloat16 or wider, within the bound.
A program may use at most 64 MiB of HBM per device.

v0:
```python
import jax
import jax.numpy as jnp
from jax import lax
from jax.sharding import PartitionSpec as P

E_DEV = 4
SEQ = 128
QB = 4
CAP = 2


DAMP = 0.1


def kron_inverse(factor):
    width = factor.shape[0]
    identity = jnp.eye(width, dtype=jnp.float32)
    damping = DAMP * jnp.trace(factor) / width + 1e-06
    lower_factor = jnp.linalg.cholesky(factor + damping * identity)
    return jax.scipy.linalg.cho_solve((lower_factor, True), identity)


def body(x_act, g_out, proj_in, proj_out, queries, cand_ids, cand_counts):
    act_rows = x_act[0]
    grad_rows = g_out[0]
    row_count = act_rows.shape[0]
    width = proj_in.shape[2]
    n_owners = lax.axis_size("dp")
    n_layers = lax.axis_size("block")
    act_proj = jnp.dot(act_rows, proj_in[0], preferred_element_type=jnp.float32).astype(
        jnp.bfloat16
    )
    grad_proj = jnp.dot(grad_rows, proj_out[0], preferred_element_type=jnp.float32).astype(
        jnp.bfloat16
    )
    contract_rows = (((0,), (0,)), ((), ()))
    part_a = lax.dot_general(act_proj, act_proj, contract_rows, preferred_element_type=jnp.float32)
    part_g = lax.dot_general(
        grad_proj, grad_proj, contract_rows, preferred_element_type=jnp.float32
    )
    factor_a, factor_g = lax.psum((part_a, part_g), "dp")
    token_total = row_count * n_owners
    inverse_a = kron_inverse(factor_a / token_total)
    inverse_g = kron_inverse(factor_g / token_total)
    act_three = act_proj.reshape(E_DEV, SEQ, width)
    grad_three = grad_proj.reshape(E_DEV, SEQ, width)
    example_grad = (
        jnp.einsum("esi,esj->eij", grad_three, act_three, preferred_element_type=jnp.float32) / SEQ
    )
    left_side = jnp.einsum("ij,ejk->eik", inverse_g, example_grad, precision=lax.Precision.HIGHEST)
    precond = jnp.einsum("eik,kl->eil", left_side, inverse_a, precision=lax.Precision.HIGHEST)
    precond = precond.reshape(E_DEV, width * width).astype(jnp.bfloat16)
    req_ids, req_counts = (
        lax.all_to_all(cand_ids, "dp", split_axis=1, concat_axis=0, tiled=True),
        lax.all_to_all(cand_counts, "dp", split_axis=1, concat_axis=0, tiled=True),
    )
    req_ids = req_ids.reshape(n_owners, CAP)
    req_counts = req_counts.reshape(n_owners)
    query_rows = queries[0]
    owned = query_rows.shape[0]
    block_count = owned // QB
    slot_live = jnp.arange(CAP)[None, :] < req_counts[:, None]
    onehot = (
        (req_ids[:, :, None] == jnp.arange(block_count)[None, None, :]) & slot_live[:, :, None]
    ).astype(jnp.float32)
    dense_part = lax.dot_general(
        query_rows,
        lax.all_gather(precond, "dp", axis=0, tiled=True),
        (((1,), (1,)), ((), ())),
        preferred_element_type=jnp.float32,
    )
    live_blocks = jnp.sum(onehot, axis=1)
    mask_full = jnp.broadcast_to(
        jnp.transpose(live_blocks)[:, None, :, None], (block_count, QB, n_owners, E_DEV)
    ).reshape(owned, n_owners * E_DEV)
    layer_part = dense_part * mask_full
    scale = 1.0 / float(width * width * n_layers) ** 0.5
    return lax.psum_scatter(layer_part * scale, "block", scatter_dimension=0, tiled=True)


def solution(mesh):
    return jax.shard_map(
        body,
        mesh=mesh,
        in_specs=(
            P("block", "dp", None),
            P("block", "dp", None),
            P("block", None, None),
            P("block", None, None),
            P("block", "dp", None),
            P("dp", None, None),
            P("dp", None),
        ),
        out_specs=P(("dp", "block"), None),
        check_vma=False,
    )
```

profile of v0, /device:TPU:0, one launch (start us, length us, event | category | flops | bytes accessed | tf_op | source)
XLA Modules:
  0.0 153.5 jit_solution(9297997313846450006)
XLA Ops:
  6.5 1.4 copy.56
  7.9 7.3 %all-to-all-start.1 = ((s32[1,8,1]{2,0,1:T(1,128)}), s32[1,8,1]{2,0,1:T(1,128)S(1)}, u32[]{:S(2)}, u32[]{:S(2)}) async-start(s32[1,8,1]{2,0,1:T(1,128)} %copy.56), calls=%async_computation.1 | async-start | bytes 8192 | tf_op jit(solution)/shard_map/all_to_all | solution.py:55
  15.3 3.7 %fusion.7 = bf16[512,64]{0,1:T(8,128)(2,1)S(1)} fusion(bf16[1,512,4096]{2,1,0:T(8,128)(2,1)} %param.10, bf16[1,4096,64]{1,2,0:T(8,128)(2,1)S(1)} %copy-done), kind=kOutput, calls=%fused_computation.7 | convolution fusion | flops 268468224 | bytes 4784128 | tf_op jit(solution)/shard_map/dot_general | solution.py:30
  19.0 0.2 fusion.33
  19.2 1.4 fusion.4
  20.6 0.2 fusion.32
  20.7 0.2 convolution_multiply_fusion
  20.9 0.7 copy.54
  21.6 38.0 %all-reduce = (f32[64,64]{0,1:T(8,128)S(1)}, f32[64,64]{0,1:T(8,128)S(1)}) all-reduce(f32[64,64]{0,1:T(8,128)S(1)} %fusion.32, f32[64,64]{0,1:T(8,128)S(1)} %fusion.33), channel_id=1, replica_groups=mesh['dp'=8,'block'=4] {'dp'}, use_global_device_ids=true, to_apply=%region_0.0 | all-reduce | flops 8192 | bytes 65536 | tf_op jit(solution)/shard_map/psum | solution.py:41
  59.6 0.6 select_reduce_fusion.2
  60.2 0.6 select_reduce_fusion.3
  62.1 5.8 %cholesky.55 = f32[64,64]{1,0:T(8,128)S(1)} custom-call(f32[64,64]{1,0:T(8,128)S(1)} %fusion.27), custom_call_target="Cholesky" | custom-call | tf_op jit(solution)/shard_map/jit(cholesky)/cholesky | solution.py:19
  68.0 0.6 compare_reduce_fusion
  68.7 0.6 fusion.24
  69.2 4.9 %custom-call.9 = f32[1,64,64]{1,2,0:T(8,128)S(1)} custom-call(f32[1,64,64]{2,1,0:T(8,128)S(1)} %fusion.24), custom_call_target="InvertDiagBlocksLowerTriangular" | custom-call | tf_op jit(solution)/shard_map/jit(_cho_solve)/triangular_solve | solution.py:20
  74.1 0.3 fusion.19
  74.4 0.2 convolution_bitcast_fusion.1
  74.6 5.8 %cholesky.44 = f32[64,64]{1,0:T(8,128)S(1)} custom-call(f32[64,64]{1,0:T(8,128)S(1)} %fusion.30), custom_call_target="Cholesky" | custom-call | tf_op jit(solution)/shard_map/jit(cholesky)/cholesky | solution.py:19
  80.5 0.6 compare_reduce_fusion.1
  81.2 0.6 fusion.23
  81.7 4.9 %custom-call.8 = f32[1,64,64]{1,2,0:T(8,128)S(1)} custom-call(f32[1,64,64]{2,1,0:T(8,128)S(1)} %fusion.23), custom_call_target="InvertDiagBlocksLowerTriangular" | custom-call | tf_op jit(solution)/shard_map/jit(_cho_solve)/triangular_solve | solution.py:20
  86.6 0.3 fusion.21
  86.9 0.2 convolution_bitcast_fusion.2
  87.1 0.4 convolution_bitcast_fusion
  87.5 0.4 convolution_convert_fusion
  88.0 30.8 %all-gather = bf16[8,4,4096]{2,1,0:T(4,128)(2,1)S(1)} all-gather(bf16[1,4,4096]{2,1,0:T(4,128)(2,1)S(1)} %reshape.60), channel_id=1, replica_groups=mesh['dp'=8,'block'=4] {'dp'}, dimensions={0}, use_global_device_ids=true | all-gather | bytes 294912 | tf_op jit(solution)/shard_map/all_gather | solution.py:68
  118.8 3.3 %all-to-all-start = ((s32[1,8,2]{2,0,1:T(1,128)}), s32[1,8,2]{2,0,1:T(1,128)S(1)}, u32[]{:S(2)}, u32[]{:S(2)}) async-start(s32[1,8,2]{2,0,1:T(1,128)} %copy.54), calls=%async_computation | async-start | bytes 8192 | tf_op jit(solution)/shard_map/all_to_all | solution.py:54
  122.2 0.2 reduce.4
  122.4 6.0 %all-to-all-done = s32[1,8,2]{2,0,1:T(1,128)S(1)} async-done(((s32[1,8,2]{2,0,1:T(1,128)}), s32[1,8,2]{2,0,1:T(1,128)S(1)}, u32[]{:S(2)}, u32[]{:S(2)}) %all-to-all-start) | async-done | bytes 96 | tf_op jit(solution)/shard_map/all_to_all | solution.py:54
  128.9 0.3 fusion.11
  129.1 0.7 copy.62
  129.9 16.8 %reduce-scatter.4.cloned.1.call-done = f32[16,32]{1,0:T(8,128)} async-done(((f32[64,32]{1,0:T(8,128)}), f32[16,32]{1,0:T(8,128)}) %reduce-scatter.4.cloned.1.call-update) | async-done | bytes 2064 | tf_op jit(solution)/shard_map/reduce_scatter | solution.py:78
  (27 shorter events, 0.9 us)
Async XLA Ops:
  6.5 8.7 %copy-start = (bf16[1,4096,64]{1,2,0:T(8,128)(2,1)S(1)}, bf16[1,4096,64]{1,2,0:T(8,128)(2,1)}, u32[]{:S(2)}) copy-start(bf16[1,4096,64]{1,2,0:T(8,128)(2,1)} %param.12) | copy-start | bytes 1572868
  6.5 12.6 %copy-start.2 = (bf16[1,4096,64]{1,2,0:T(8,128)(2,1)S(1)}, bf16[1,4096,64]{1,2,0:T(8,128)(2,1)}, u32[]{:S(2)}) copy-start(bf16[1,4096,64]{1,2,0:T(8,128)(2,1)} %param.13) | copy-start | bytes 1572868
  7.9 110.8 %all-to-all-start.1 = ((s32[1,8,1]{2,0,1:T(1,128)}), s32[1,8,1]{2,0,1:T(1,128)S(1)}, u32[]{:S(2)}, u32[]{:S(2)}) async-start(s32[1,8,1]{2,0,1:T(1,128)} %copy.56), calls=%async_computation.1 | async-start | bytes 8192 | tf_op jit(solution)/shard_map/all_to_all | solution.py:55
  15.2 3.9 %copy-start.1 = (bf16[1,512,4096]{2,1,0:T(8,128)(2,1)S(1)}, bf16[1,512,4096]{2,1,0:T(8,128)(2,1)}, u32[]{:S(2)}) copy-start(bf16[1,512,4096]{2,1,0:T(8,128)(2,1)} %param.11) | copy-start | bytes 12582916
  15.2 5.7 %copy-start.4 = (s32[1,8,2]{1,2,0:T(2,128)S(1)}, s32[1,8,2]{1,2,0:T(2,128)}, u32[]{:S(2)}) copy-start(s32[1,8,2]{1,2,0:T(2,128)} %param.15) | copy-start | bytes 196
  19.2 109.7 %copy-start.3 = (bf16[1,64,4096]{2,1,0:T(8,128)(2,1)S(1)}, bf16[1,64,4096]{2,1,0:T(8,128)(2,1)}, u32[]{:S(2)}) copy-start(bf16[1,64,4096]{2,1,0:T(8,128)(2,1)} %param.14) | copy-start | bytes 1572868
  118.8 9.7 %all-to-all-start = ((s32[1,8,2]{2,0,1:T(1,128)}), s32[1,8,2]{2,0,1:T(1,128)S(1)}, u32[]{:S(2)}, u32[]{:S(2)}) async-start(s32[1,8,2]{2,0,1:T(1,128)} %copy.54), calls=%async_computation | async-start | bytes 8192 | tf_op jit(solution)/shard_map/all_to_all | solution.py:54
  122.1 24.5 %reduce-scatter.4.cloned.1.call-start = ((), (), s32[]{:S(2)}) async-start(), calls=%async_computation.3 | async-start | bytes 40960 | tf_op jit(solution)/shard_map/reduce_scatter | solution.py:78
Sparse Core Ops, SparseCore 0:
  130.0 16.5 reduce-scatter.3
where the time goes:
time: 154 us; the launch traced here: 153 us
  blocking collectives  68.7 us (45%)
  other arithmetic  25.5 us (17%)
  waiting for transfers between devices  22.8 us (15%)
  between operations  14.8 us (10%)
  starting transfers between devices  10.6 us (7%)
  matrix products  7.44 us (5%)
  local copies, waits for them, and re-layouts  3.46 us (2%)
    psum x1, blocking collectives, body(): factor_a, factor_g = lax.psum((part_a, part_g), 'dp')  38 us
    all_gather x1, blocking collectives, body(): lax.all_gather(precond, 'dp', axis=0, tiled=True)  30.8 us
    reduce_scatter x1, waiting for transfers between devices, body(): lax.psum_scatter(layer_part * scale, 'block', scatter_dimension=0, tiled=...  16.8 us
    another operation x6, other arithmetic, kron_inverse(): lower_factor = jnp.linalg.cholesky(factor + damping * identity)  13 us
    another operation x4, other arithmetic, kron_inverse(): return jax.scipy.linalg.cho_solve((lower_factor, True), identity)  10.9 us
    all_to_all x1, starting transfers between devices, body(): lax.all_to_all(cand_counts, 'dp', split_axis=1, concat_axis=0, tiled=True)  7.28 us
    all_to_all x1, waiting for transfers between devices, body(): lax.all_to_all(cand_ids, 'dp', split_axis=1, concat_axis=0, tiled=True)  6.03 us
    dot_general x1, matrix products, body(): jnp.dot(act_rows, proj_in[0], preferred_element_type=jnp.float32)  3.73 us
  transfers between devices with their start and end apart: 3, of which 2 were waited for; matrix products, arithmetic and copies ran while one was open for 22% of the time, Pallas kernels for 0%

commit v1 on v0

v1 whole, which is shorter than its diff:
```python
import functools

import jax
import jax.numpy as jnp
from jax import lax
from jax.experimental import pallas as pl
from jax.experimental.pallas import tpu as pltpu
from jax.sharding import PartitionSpec as P

E_DEV = 4
SEQ = 128
QB = 4
CAP = 2
DAMP = 0.1
MESH = pl.DeviceIdType.MESH
HIGHEST = lax.Precision.HIGHEST


def dot(lhs, rhs, dims=(1, 0), precision=None):
    return lax.dot_general(
        lhs,
        rhs,
        (((dims[0],), (dims[1],)), ((), ())),
        preferred_element_type=jnp.float32,
        precision=precision,
    )


def kron_inverses(packed, width):
    shape = packed.shape
    lane_all = lax.broadcasted_iota(jnp.int32, shape, 1)
    first = lane_all < width
    lane = jnp.where(first, lane_all, lane_all - width)
    sub = lax.broadcasted_iota(jnp.int32, shape, 0)
    diag = jnp.sum(jnp.where(lane == sub, packed, 0.0), axis=0, keepdims=True)
    first_row = first[0:1]
    trace_a = jnp.sum(jnp.where(first_row, diag, 0.0), axis=1, keepdims=True)
    trace_g = jnp.sum(jnp.where(first_row, 0.0, diag), axis=1, keepdims=True)
    damping = DAMP * jnp.where(first_row, trace_a, trace_g) / width + 1e-06
    mat = packed + jnp.where(lane == sub, damping, 0.0)
    lane_row = lane[0:1]

    def column(k):
        col_a = jnp.broadcast_to(mat[:, k : k + 1], shape)
        col_g = jnp.broadcast_to(mat[:, width + k : width + k + 1], shape)
        return jnp.where(first, col_a, col_g)

    for k in range(0, width, 2):
        col0, col1 = column(k), column(k + 1)
        p00, p01, p11 = col0[k : k + 1], col0[k + 1 : k + 2], col1[k + 1 : k + 2]
        inv_det = 1.0 / (p00 * p11 - p01 * p01)
        at0, at1 = lane_row == k, lane_row == k + 1
        row0 = jnp.where(at0, 1.0, jnp.where(at1, 0.0, mat[k : k + 1]))
        row1 = jnp.where(at1, 1.0, jnp.where(at0, 0.0, mat[k + 1 : k + 2]))
        new0 = (p11 * row0 - p01 * row1) * inv_det
        new1 = (p00 * row1 - p01 * row0) * inv_det
        in0, in1 = sub == k, sub == k + 1
        keep = jnp.where((lane == k) | (lane == k + 1) | in0 | in1, 0.0, mat)
        mul0 = jnp.where(in0, -1.0, jnp.where(in1, 0.0, col0))
        mul1 = jnp.where(in1, -1.0, jnp.where(in0, 0.0, col1))
        mat = keep - mul0 * new0 - mul1 * new1
    return mat


def kernel(
    n, layers, x_hbm, g_hbm, pin_hbm, pout_hbm, q_hbm, ids_ref, counts_ref, out_ref,
    xbuf, gbuf, pin, pout, qbuf, fsend, frecv, fred, fall, tg_ref, flat_src, flat, tbuf,
    part, sbuf, load_x, load_g, load_p, send1, recv1, send2, recv2, send_a, recv_a,
    send_b, recv_b, send_s, recv_s,
):
    me = lax.axis_index("dp")
    layer = lax.axis_index("block")
    width = pin.shape[0]
    lanes = 2 * width
    owned = qbuf.shape[0]
    rows = width // n
    chunks = 16 // E_DEV
    chunk = tbuf.shape[2]

    loads = []
    pin_copy = pltpu.make_async_copy(pin_hbm, pin, load_p.at[0])
    pout_copy = pltpu.make_async_copy(pout_hbm, pout, load_p.at[1])
    q_copy = pltpu.make_async_copy(q_hbm, qbuf, load_p.at[2])
    pin_copy.start()
    pout_copy.start()
    for e in range(E_DEV):
        span = pl.ds(e * SEQ, SEQ)
        x_copy = pltpu.make_async_copy(x_hbm.at[span], xbuf.at[e], load_x.at[e])
        g_copy = pltpu.make_async_copy(g_hbm.at[span], gbuf.at[e], load_g.at[e])
        x_copy.start()
        g_copy.start()
        loads.append((x_copy, g_copy))
    q_copy.start()

    barrier = pltpu.get_barrier_semaphore()
    for o in range(1, n):
        pl.semaphore_signal(
            barrier, inc=1, device_id=(lax.rem(me + o, n), layer), device_id_type=MESH
        )
    for o in range(1, layers):
        pl.semaphore_signal(
            barrier, inc=1, device_id=(me, lax.rem(layer + o, layers)), device_id_type=MESH
        )

    lane_q = lax.broadcasted_iota(jnp.int32, (8, lanes), 1) // QB
    for p in range(n):
        live = jnp.zeros((8, lanes), jnp.float32)
        for s in range(CAP):
            wanted = jnp.where(s < counts_ref[0, p], ids_ref[s, p], -1)
            live = jnp.where(lane_q == wanted, 1.0, live)
        fsend[p, 8 * pl.cdiv(rows, 8) :, :] = live

    pin_copy.wait()
    pout_copy.wait()
    grams = jnp.zeros((lanes, lanes), jnp.float32)
    for e in range(E_DEV):
        loads[e][0].wait()
        act = dot(xbuf[e], pin[...], (1, 1))
        loads[e][1].wait()
        grad = dot(gbuf[e], pout[...], (1, 1))
        both = jnp.concatenate([act, grad], axis=1).astype(jnp.bfloat16)
        gram = dot(both, both, (0, 0))
        tg_ref[e * width : (e + 1) * width, :] = gram[width:, :width] * (1.0 / SEQ)
        grams = grams + gram
    lane_sq = lax.broadcasted_iota(jnp.int32, (width, lanes), 1)
    first = lane_sq < width
    factors = jnp.where(first, grams[:width], grams[width:])
    for p in range(n):
        fsend[p, 0:rows, :] = factors[p * rows : (p + 1) * rows]

    pl.semaphore_wait(barrier, n - 1 + layers - 1)

    def to_dp(src, dst, send, recv, peer):
        return pltpu.make_async_remote_copy(
            src_ref=src, dst_ref=dst, send_sem=send, recv_sem=recv,
            device_id=(peer, layer), device_id_type=MESH,
        )

    first_copies = []
    for o in range(1, n):
        peer = lax.rem(me + o, n)
        copy = to_dp(fsend.at[peer], frecv.at[me], send1.at[o], recv1.at[o], peer)
        copy.start()
        first_copies.append(copy)
    frecv[pl.ds(me, 1)] = fsend[pl.ds(me, 1)]
    for copy in first_copies:
        copy.wait_recv()
    total = frecv[0, 0:rows, :]
    for d in range(1, n):
        total = total + frecv[d, 0:rows, :]
    total = total * (1.0 / (n * E_DEV * SEQ))
    fred[0:rows, :] = total

    second_copies = []
    for o in range(1, n):
        peer = lax.rem(me + o, n)
        copy = to_dp(fred, fall.at[me], send2.at[o], recv2.at[o], peer)
        copy.start()
        second_copies.append(copy)
    fall[pl.ds(me, 1)] = fred[...][None]
    for copy in second_copies:
        copy.wait_recv()

    packed = jnp.concatenate([fall[d, 0:rows, :] for d in range(n)], axis=0)
    inverses = kron_inverses(packed, width)
    swapped = pltpu.roll(inverses, width, 1)
    inverse_a2 = jnp.where(first, inverses, swapped)
    inverse_g = swapped[:, :width]
    right = dot(tg_ref[...], inverse_a2, precision=HIGHEST)
    for e in range(E_DEV):
        span = slice(e * width, (e + 1) * width)
        flat_src[span, :] = dot(inverse_g, right[span], precision=HIGHEST)
    even = lax.broadcasted_iota(jnp.int32, (E_DEV, lanes), 1) < width
    per_chunk = chunk // lanes
    for m in range(width // 2):
        lo = flat_src[pl.ds(2 * m, E_DEV, stride=width), :]
        hi = flat_src[pl.ds(2 * m + 1, E_DEV, stride=width), :]
        c, at = m // per_chunk, (m % per_chunk) * lanes
        flat[c * E_DEV : (c + 1) * E_DEV, at : at + lanes] = jnp.where(even, lo, hi)
    tbuf[pl.ds(me, 1)] = flat[...].astype(jnp.bfloat16)[None]

    partner = me + 1 - 2 * lax.rem(me, 2)
    half = n // 2
    across = [to_dp(tbuf.at[me], tbuf.at[me], send_b.at[0], recv_b.at[0], partner)]
    along = []
    for o in range(1, half):
        peer = lax.rem(me + 2 * o, n)
        along.append(to_dp(tbuf.at[me], tbuf.at[me], send_a.at[o], recv_a.at[o], peer))
        along[-1].start()
    across[0].start()
    for o in range(1, half):
        source = lax.rem(me + n - 2 * o, n)
        to_dp(
            tbuf.at[source], tbuf.at[source], send_a.at[o], recv_a.at[o], partner
        ).wait_recv()
        across.append(
            to_dp(tbuf.at[source], tbuf.at[source], send_b.at[o], recv_b.at[o], partner)
        )
        across[-1].start()
    q_copy.wait()
    for o in range(half):
        source = lax.rem(partner + n - 2 * o, n)
        to_dp(
            tbuf.at[source], tbuf.at[source], send_b.at[o], recv_b.at[o], partner
        ).wait_recv()

    group = lax.broadcasted_iota(jnp.int32, (n * 16, owned), 0) % 16 // E_DEV
    got = jnp.zeros((n * 16, owned), jnp.float32)
    for c in range(chunks):
        queries = qbuf[:, c * chunk : (c + 1) * chunk]
        term = dot(tbuf[...].reshape(n * 16, chunk), queries, (1, 1))
        got = jnp.where(group == c, term, got)
    live_rows = []
    for d in range(n):
        tile = frecv[d, 8 * pl.cdiv(rows, 8) :, :][:, :owned]
        live_rows += [tile, tile]
    got = got * jnp.concatenate(live_rows, axis=0)
    out_lanes = part.shape[1]
    shape = (n * 16, out_lanes)
    src = lax.broadcasted_iota(jnp.int32, shape, 0)
    pick = (src // 16) * E_DEV + src % E_DEV == lax.broadcasted_iota(jnp.int32, shape, 1)
    scores = dot(got, pick.astype(jnp.float32), (0, 0), precision=HIGHEST)
    scale = 1.0 / float(width * width * layers) ** 0.5
    part[...] = scores * scale

    share = owned // layers
    last_copies = []
    for o in range(1, layers):
        peer = lax.rem(layer + o, layers)
        copy = pltpu.make_async_remote_copy(
            src_ref=part.at[pl.ds(pl.multiple_of(peer * share, 8), share)],
            dst_ref=sbuf.at[o],
            send_sem=send_s.at[o],
            recv_sem=recv_s.at[o],
            device_id=(me, peer),
            device_id_type=MESH,
        )
        copy.start()
        last_copies.append(copy)
    result = part[pl.ds(pl.multiple_of(layer * share, 8), share), :]
    for o, copy in enumerate(last_copies, 1):
        copy.wait_recv()
        result = result + sbuf[o]
    out_ref[...] = result[:, : out_ref.shape[1]]
    for copy in first_copies + second_copies + along + across + last_copies:
        copy.wait_send()


def body(x_act, g_out, proj_in, proj_out, queries, cand_ids, cand_counts):
    n = lax.axis_size("dp")
    layers = lax.axis_size("block")
    depth = x_act.shape[2]
    width = proj_in.shape[2]
    owned = queries.shape[1]
    rows = width // n
    pad = 8 * pl.cdiv(rows, 8)
    chunk = width * width * E_DEV // 16
    out_lanes = 128 * pl.cdiv(n * E_DEV, 128)
    bf16, f32 = jnp.bfloat16, jnp.float32
    sems = pltpu.SemaphoreType.DMA
    vmem = pltpu.VMEM
    return pl.pallas_call(
        functools.partial(kernel, n, layers),
        out_shape=jax.ShapeDtypeStruct((owned // layers, n * E_DEV), f32),
        in_specs=[pl.BlockSpec(memory_space=pltpu.HBM)] * 5
        + [pl.BlockSpec(memory_space=pltpu.SMEM)] * 2,
        out_specs=pl.BlockSpec(memory_space=pltpu.VMEM),
        scratch_shapes=[
            vmem((E_DEV, SEQ, depth), bf16),
            vmem((E_DEV, SEQ, depth), bf16),
            vmem((width, depth), bf16),
            vmem((width, depth), bf16),
            vmem((owned, width * width), bf16),
            vmem((n, pad + 8, 2 * width), f32),
            vmem((n, pad + 8, 2 * width), f32),
            vmem((pad, 2 * width), f32),
            vmem((n, pad, 2 * width), f32),
            vmem((E_DEV * width, width), f32),
            vmem((E_DEV * width, 2 * width), f32),
            vmem((16, chunk), f32),
            vmem((n, 16, chunk), bf16),
            vmem((owned, out_lanes), f32),
            vmem((layers, owned // layers, out_lanes), f32),
            sems((E_DEV,)),
            sems((E_DEV,)),
            sems((3,)),
            sems((n,)),
            sems((n,)),
            sems((n,)),
            sems((n,)),
            sems((n // 2,)),
            sems((n // 2,)),
            sems((n // 2,)),
            sems((n // 2,)),
            sems((layers,)),
            sems((layers,)),
        ],
        compiler_params=pltpu.CompilerParams(
            collective_id=0, has_side_effects=True, vmem_limit_bytes=40 * 1024 * 1024
        ),
        name="influence",
    )(
        x_act[0],
        g_out[0],
        jnp.swapaxes(proj_in, 1, 2)[0],
        jnp.swapaxes(proj_out, 1, 2)[0],
        queries[0],
        jnp.swapaxes(cand_ids, 1, 2)[0],
        cand_counts,
    )


def solution(mesh):
    return jax.shard_map(
        body,
        mesh=mesh,
        in_specs=(
            P("block", "dp", None),
            P("block", "dp", None),
            P("block", None, None),
            P("block", None, None),
            P("block", "dp", None),
            P("dp", None, None),
            P("dp", None),
        ),
        out_specs=P(("dp", "block"), None),
        check_vma=False,
    )
```

time: 154 us -> 45.5 us (0.30)
  blocking collectives: 68.7 us -> 0 us
  Pallas kernels: 0 us -> 35.7 us
  other arithmetic: 25.5 us -> 0 us
  waiting for transfers between devices: 22.8 us -> 0 us
  between operations: 14.8 us -> 0.02 us
  starting transfers between devices: 10.6 us -> 0 us
  matrix products: 7.44 us -> 0 us
  local copies, waits for them, and re-layouts: 3.46 us -> 9.43 us
    psum x1 -> x0, blocking collectives: 38 us -> none  [body(): factor_a, factor_g = lax.psum((part_a, part_g), 'dp')]
    pallas_call x0 -> x1, Pallas kernels: none -> 35.7 us  [body(): pl.pallas_call(functools.partial(kernel, n, layers), out_shape=jax.ShapeD...]
    all_gather x1 -> x0, blocking collectives: 30.8 us -> none  [body(): lax.all_gather(precond, 'dp', axis=0, tiled=True)]
    another operation x10 -> x0, other arithmetic: 23.9 us -> none  [the longest x6 13 us: kron_inverse(): lower_factor = jnp.linalg.cholesky(factor + damping * identity)]
    reduce_scatter x1 -> x0, waiting for transfers between devices: 16.8 us -> none  [body(): lax.psum_scatter(layer_part * scale, 'block', scatter_dimension=0, tiled=...]
    all_to_all x2 -> x0, starting transfers between devices: 10.6 us -> none  [the longest x1 7.28 us: body(): lax.all_to_all(cand_counts, 'dp', split_axis=1, concat_axis=0, tiled=True)]
    unnamed x14 -> x15, local copies, waits for them, and re-layouts: 1.59 us -> 9.43 us
    dot_general x8 -> x0, matrix products: 6.61 us -> none  [the longest x1 3.73 us: body(): jnp.dot(act_rows, proj_in[0], preferred_element_type=jnp.float32)]
  transfers between devices with their start and end apart: 3 -> 0, of which waited for: 2 -> 0; matrix products, arithmetic and copies ran while one was open for 22% -> 0% of each run, Pallas kernels for 0% -> 0%
where the time goes in v1:
time: 45.5 us; the launch traced here: 45.2 us
  Pallas kernels  35.7 us (78%)
  local copies, waits for them, and re-layouts  9.43 us (21%)
    pallas_call x1, Pallas kernels, body(): pl.pallas_call(functools.partial(kernel, n, layers), out_shape=jax.ShapeD...  35.7 us
    unnamed x15, local copies, waits for them, and re-layouts  9.43 us

profile of v1, /device:TPU:0, one launch (start us, length us, event | category | flops | bytes accessed | tf_op | source)
XLA Modules:
  0.0 45.2 jit_solution(3855251937159651382)
XLA Ops:
  0.0 0.0 copy-start
  0.0 2.2 %copy-done = bf16[1,512,4096]{2,1,0:T(8,128)(2,1)S(1)} copy-done((bf16[1,512,4096]{2,1,0:T(8,128)(2,1)S(1)}, bf16[1,512,4096]{2,1,0:T(8,128)(2,1)}, u32[]{:S(2)}) %copy-start) | copy-done | bytes 4194328
  2.2 0.0 copy-start.1
  2.2 2.2 %copy-done.1 = bf16[1,512,4096]{2,1,0:T(8,128)(2,1)S(1)} copy-done((bf16[1,512,4096]{2,1,0:T(8,128)(2,1)S(1)}, bf16[1,512,4096]{2,1,0:T(8,128)(2,1)}, u32[]{:S(2)}) %copy-start.1) | copy-done | bytes 4194328
  4.4 0.0 copy-start.2
  4.4 1.0 %copy-done.2 = bf16[1,4096,64]{1,2,0:T(8,128)(2,1)S(1)} copy-done((bf16[1,4096,64]{1,2,0:T(8,128)(2,1)S(1)}, bf16[1,4096,64]{1,2,0:T(8,128)(2,1)}, u32[]{:S(2)}) %copy-start.2) | copy-done | bytes 524312
  5.4 0.0 copy-start.3
  5.4 1.0 %copy-done.3 = bf16[1,4096,64]{1,2,0:T(8,128)(2,1)S(1)} copy-done((bf16[1,4096,64]{1,2,0:T(8,128)(2,1)S(1)}, bf16[1,4096,64]{1,2,0:T(8,128)(2,1)}, u32[]{:S(2)}) %copy-start.3) | copy-done | bytes 524312
  6.5 0.0 copy-start.4
  6.5 1.0 %copy-done.4 = bf16[1,64,4096]{2,1,0:T(8,128)(2,1)S(1)} copy-done((bf16[1,64,4096]{2,1,0:T(8,128)(2,1)S(1)}, bf16[1,64,4096]{2,1,0:T(8,128)(2,1)}, u32[]{:S(2)}) %copy-start.4) | copy-done | bytes 524312
  7.5 0.0 copy-start.5
  7.5 0.7 %copy-done.5 = s32[1,8,2]{1,2,0:T(2,128)S(1)} copy-done((s32[1,8,2]{1,2,0:T(2,128)S(1)}, s32[1,8,2]{1,2,0:T(2,128)}, u32[]{:S(2)}) %copy-start.5) | copy-done | bytes 88
  8.2 0.0 copy-start.6
  8.2 0.7 %copy-done.6 = s32[1,8]{1,0:T(1,128)S(1)} copy-done((s32[1,8]{1,0:T(1,128)S(1)}, s32[1,8]{1,0:T(1,128)}, u32[]{:S(2)}) %copy-start.6) | copy-done | bytes 56
  8.8 35.7 %influence.1 = f32[16,32]{1,0:T(8,128)S(1)} custom-call(bf16[512,4096]{1,0:T(8,128)(2,1)S(1)} %bitcast.12, bf16[512,4096]{1,0:T(8,128)(2,1)S(1)} %bitcast.13, bf16[64,4096]{1,0:T(8,128)(2,1)S(1)} %bitcast.14, bf16[64,4096]{1,0:T(8,128)(2,1)S(1)} %bitcast.15, bf16[64,4096]{1,0:T(8,128)(2,1)S(1)} %bitcast.16, s32[2,8]{1,0:T(2,128)S(1)} %bitcast.17, ...), custom_call_target="tpu_custom_call" | custom-call | tf_op jit(solution)/shard_map/influence/pallas_call | solution.py:262
  44.6 0.6 %copy.9 = f32[16,32]{1,0:T(8,128)} copy(f32[16,32]{1,0:T(8,128)S(1)} %influence.1) | data formatting | bytes 4096
Async XLA Ops:
  0.0 2.2 %copy-start = (bf16[1,512,4096]{2,1,0:T(8,128)(2,1)S(1)}, bf16[1,512,4096]{2,1,0:T(8,128)(2,1)}, u32[]{:S(2)}) copy-start(bf16[1,512,4096]{2,1,0:T(8,128)(2,1)} %param.7) | copy-start | bytes 12582916
  2.2 2.2 %copy-start.1 = (bf16[1,512,4096]{2,1,0:T(8,128)(2,1)S(1)}, bf16[1,512,4096]{2,1,0:T(8,128)(2,1)}, u32[]{:S(2)}) copy-start(bf16[1,512,4096]{2,1,0:T(8,128)(2,1)} %param.8) | copy-start | bytes 12582916
  4.4 1.0 %copy-start.2 = (bf16[1,4096,64]{1,2,0:T(8,128)(2,1)S(1)}, bf16[1,4096,64]{1,2,0:T(8,128)(2,1)}, u32[]{:S(2)}) copy-start(bf16[1,4096,64]{1,2,0:T(8,128)(2,1)} %param.9) | copy-start | bytes 1572868
  5.4 1.0 %copy-start.3 = (bf16[1,4096,64]{1,2,0:T(8,128)(2,1)S(1)}, bf16[1,4096,64]{1,2,0:T(8,128)(2,1)}, u32[]{:S(2)}) copy-start(bf16[1,4096,64]{1,2,0:T(8,128)(2,1)} %param.10) | copy-start | bytes 1572868
  6.5 1.0 %copy-start.4 = (bf16[1,64,4096]{2,1,0:T(8,128)(2,1)S(1)}, bf16[1,64,4096]{2,1,0:T(8,128)(2,1)}, u32[]{:S(2)}) copy-start(bf16[1,64,4096]{2,1,0:T(8,128)(2,1)} %param.11) | copy-start | bytes 1572868
  7.5 0.7 %copy-start.5 = (s32[1,8,2]{1,2,0:T(2,128)S(1)}, s32[1,8,2]{1,2,0:T(2,128)}, u32[]{:S(2)}) copy-start(s32[1,8,2]{1,2,0:T(2,128)} %param.12) | copy-start | bytes 196
  8.2 0.7 %copy-start.6 = (s32[1,8]{1,0:T(1,128)S(1)}, s32[1,8]{1,0:T(1,128)}, u32[]{:S(2)}) copy-start(s32[1,8]{1,0:T(1,128)} %counts_ref.1) | copy-start | bytes 100

commit v2 on v1

--- a/solution.py
+++ b/solution.py
@@ -296,7 +296,7 @@
             sems((layers,)),
         ],
         compiler_params=pltpu.CompilerParams(
-            collective_id=0, has_side_effects=True, vmem_limit_bytes=40 * 1024 * 1024
+            collective_id=0, has_side_effects=True, vmem_limit_bytes=64 * 1024 * 1024 - 131072
         ),
         name="influence",
     )(

time: 45.5 us -> 39.7 us (0.87)
  local copies, waits for them, and re-layouts: 9.43 us -> 1.3 us
  Pallas kernels: 35.7 us -> 38.1 us
    unnamed x15 -> x1, local copies, waits for them, and re-layouts: 9.43 us -> 1.3 us
    pallas_call x1, Pallas kernels: 35.7 us -> 38.1 us  [body(): pl.pallas_call(functools.partial(kernel, n, layers), out_shape=jax.ShapeD...]
where the time goes in v2:
time: 39.7 us; the launch traced here: 39.4 us
  Pallas kernels  38.1 us (96%)
  local copies, waits for them, and re-layouts  1.3 us (3%)
    pallas_call x1, Pallas kernels, body(): pl.pallas_call(functools.partial(kernel, n, layers), out_shape=jax.ShapeD...  38.1 us
    unnamed x1, local copies, waits for them, and re-layouts  1.3 us

profile of v2, /device:TPU:0, one launch (start us, length us, event | category | flops | bytes accessed | tf_op | source)
XLA Modules:
  0.0 39.4 jit_solution(4449114098825660496)
XLA Ops:
  0.0 38.1 %influence.1 = f32[16,32]{1,0:T(8,128)} custom-call(bf16[512,4096]{1,0:T(8,128)(2,1)} %bitcast.12, bf16[512,4096]{1,0:T(8,128)(2,1)} %bitcast.13, bf16[64,4096]{1,0:T(8,128)(2,1)} %bitcast.14, bf16[64,4096]{1,0:T(8,128)(2,1)} %bitcast.15, bf16[64,4096]{1,0:T(8,128)(2,1)} %bitcast.16, s32[2,8]{1,0:T(2,128)} %bitcast.17, s32[1,8]{1,0:T(1,128)} %counts_ref.1), custom_call_target="tpu_custom_call" | custom-call | tf_op jit(solution)/shard_map/influence/pallas_call | solution.py:262
  38.2 1.3 %copy.9 = f32[16,32]{1,0:T(8,128)} copy(f32[16,32]{1,0:T(8,128)} %influence.1) | data formatting | bytes 4096

commit v3 on v2

--- a/solution.py
+++ b/solution.py
@@ -45,8 +45,10 @@
         col_g = jnp.broadcast_to(mat[:, width + k : width + k + 1], shape)
         return jnp.where(first, col_a, col_g)
 
+    col0, col1 = column(0), column(1)
     for k in range(0, width, 2):
-        col0, col1 = column(k), column(k + 1)
+        after = [j for j in (k + 2, k + 3) if j < width]
+        stale = [column(j) for j in after]
         p00, p01, p11 = col0[k : k + 1], col0[k + 1 : k + 2], col1[k + 1 : k + 2]
         inv_det = 1.0 / (p00 * p11 - p01 * p01)
         at0, at1 = lane_row == k, lane_row == k + 1
@@ -58,7 +60,15 @@
         keep = jnp.where((lane == k) | (lane == k + 1) | in0 | in1, 0.0, mat)
         mul0 = jnp.where(in0, -1.0, jnp.where(in1, 0.0, col0))
         mul1 = jnp.where(in1, -1.0, jnp.where(in0, 0.0, col1))
+        fresh = []
+        for j, old in zip(after, stale):
+            c0, c1 = col0[j : j + 1], col1[j : j + 1]
+            n0 = (p11 * c0 - p01 * c1) * inv_det
+            n1 = (p00 * c1 - p01 * c0) * inv_det
+            fresh.append(jnp.where(in0 | in1, 0.0, old) - mul0 * n0 - mul1 * n1)
         mat = keep - mul0 * new0 - mul1 * new1
+        if fresh:
+            col0, col1 = fresh
     return mat
 
 

time: 39.7 us -> 37.9 us (0.955)
  Pallas kernels: 38.1 us -> 36.4 us
    pallas_call x1, Pallas kernels: 38.1 us -> 36.4 us  [body(): pl.pallas_call(functools.partial(kernel, n, layers), out_shape=jax.ShapeD...]
where the time goes in v3:
time: 37.9 us; the launch traced here: 37.7 us
  Pallas kernels  36.4 us (96%)
  local copies, waits for them, and re-layouts  1.3 us (3%)
    pallas_call x1, Pallas kernels, body(): pl.pallas_call(functools.partial(kernel, n, layers), out_shape=jax.ShapeD...  36.4 us
    unnamed x1, local copies, waits for them, and re-layouts  1.3 us

profile of v3, /device:TPU:0, one launch (start us, length us, event | category | flops | bytes accessed | tf_op | source)
XLA Modules:
  0.0 37.7 jit_solution(8487727573947389278)
XLA Ops:
  0.0 36.4 %influence.1 = f32[16,32]{1,0:T(8,128)} custom-call(bf16[512,4096]{1,0:T(8,128)(2,1)} %bitcast.12, bf16[512,4096]{1,0:T(8,128)(2,1)} %bitcast.13, bf16[64,4096]{1,0:T(8,128)(2,1)} %bitcast.14, bf16[64,4096]{1,0:T(8,128)(2,1)} %bitcast.15, bf16[64,4096]{1,0:T(8,128)(2,1)} %bitcast.16, s32[2,8]{1,0:T(2,128)} %bitcast.17, s32[1,8]{1,0:T(1,128)} %counts_ref.1), custom_call_target="tpu_custom_call" | custom-call | tf_op jit(solution)/shard_map/influence/pallas_call | solution.py:272
  36.4 1.3 %copy.9 = f32[16,32]{1,0:T(8,128)} copy(f32[16,32]{1,0:T(8,128)} %influence.1) | data formatting | bytes 4096

commit v4 on v3

--- a/solution.py
+++ b/solution.py
@@ -191,22 +191,20 @@
 
     partner = me + 1 - 2 * lax.rem(me, 2)
     half = n // 2
-    across = [to_dp(tbuf.at[me], tbuf.at[me], send_b.at[0], recv_b.at[0], partner)]
-    along = []
+    across, along = [], []
     for o in range(1, half):
         peer = lax.rem(me + 2 * o, n)
         along.append(to_dp(tbuf.at[me], tbuf.at[me], send_a.at[o], recv_a.at[o], peer))
         along[-1].start()
-    across[0].start()
+    for o in range(half):
+        peer = lax.rem(partner + 2 * o, n)
+        across.append(to_dp(tbuf.at[me], tbuf.at[me], send_b.at[o], recv_b.at[o], peer))
+        across[-1].start()
     for o in range(1, half):
         source = lax.rem(me + n - 2 * o, n)
         to_dp(
             tbuf.at[source], tbuf.at[source], send_a.at[o], recv_a.at[o], partner
         ).wait_recv()
-        across.append(
-            to_dp(tbuf.at[source], tbuf.at[source], send_b.at[o], recv_b.at[o], partner)
-        )
-        across[-1].start()
     q_copy.wait()
     for o in range(half):
         source = lax.rem(partner + n - 2 * o, n)

time: 37.9 us -> 36.2 us (0.955)
  Pallas kernels: 36.4 us -> 34.6 us
    pallas_call x1, Pallas kernels: 36.4 us -> 34.6 us  [body(): pl.pallas_call(functools.partial(kernel, n, layers), out_shape=jax.ShapeD...]
where the time goes in v4:
time: 36.2 us; the launch traced here: 35.9 us
  Pallas kernels  34.6 us (96%)
  local copies, waits for them, and re-layouts  1.3 us (4%)
    pallas_call x1, Pallas kernels, body(): pl.pallas_call(functools.partial(kernel, n, layers), out_shape=jax.ShapeD...  34.6 us
    unnamed x1, local copies, waits for them, and re-layouts  1.3 us

profile of v4, /device:TPU:0, one launch (start us, length us, event | category | flops | bytes accessed | tf_op | source)
XLA Modules:
  0.0 35.9 jit_solution(6487225608259173904)
XLA Ops:
  0.0 34.6 %influence.1 = f32[16,32]{1,0:T(8,128)} custom-call(bf16[512,4096]{1,0:T(8,128)(2,1)} %bitcast.12, bf16[512,4096]{1,0:T(8,128)(2,1)} %bitcast.13, bf16[64,4096]{1,0:T(8,128)(2,1)} %bitcast.14, bf16[64,4096]{1,0:T(8,128)(2,1)} %bitcast.15, bf16[64,4096]{1,0:T(8,128)(2,1)} %bitcast.16, s32[2,8]{1,0:T(2,128)} %bitcast.17, s32[1,8]{1,0:T(1,128)} %counts_ref.1), custom_call_target="tpu_custom_call" | custom-call | tf_op jit(solution)/shard_map/influence/pallas_call | solution.py:270
  34.6 1.3 %copy.9 = f32[16,32]{1,0:T(8,128)} copy(f32[16,32]{1,0:T(8,128)} %influence.1) | data formatting | bytes 4096
